TPU v7x, 128 devices: a whole 4x4x4 slice. The times are simulated.
128 devices in a mesh: expert: 4 (over y), feat: 32 (over x, z, core).
Axes of the slice: x: 4, y: 4, z: 4, core: 2. Of those that a mesh axis runs over, the one named last changes fastest.
Arguments:
- tokens: bfloat16 [1024, 4096], P(('expert', 'feat')), may hold values from -6 to 6
- expert_ids: int32 [1024, 2], P(('expert', 'feat')), may hold values from 0 to 7, as said below
- route_weights: bfloat16 [1024, 2], P(('expert', 'feat')), may hold values from 0.099609375 to 1
- gate_proj: bfloat16 [4096, 28672], P(None, ('expert', 'feat')), may hold values from -0.09375 to 0.09375
- up_proj: bfloat16 [4096, 28672], P(None, ('expert', 'feat')), may hold values from -0.09375 to 0.09375
- down_proj: bfloat16 [28672, 4096], P(('expert', 'feat')), may hold values from -0.046875 to 0.046875
- enc_weight: float32 [4096, 32768], P(None, ('expert', 'feat')), may hold values from -0.09375 to 0.09375
- enc_bias: float32 [32768], P(('expert', 'feat')), may hold values from -3 to 3
- log_threshold: float32 [32768], P(('expert', 'feat')), may hold values from -2.3 to 0
- dec_weight: float32 [32768, 4096], P(('expert', 'feat')), may hold values from -0.046875 to 0.046875
Outputs:
- grad_encoder: float32 [4096, 32768], P(None, ('expert', 'feat'))
- grad_decoder: float32 [32768, 4096], P(('expert', 'feat'))
- grad_bias: float32 [32768], P(('expert', 'feat'))
- grad_threshold: float32 [32768], P(('expert', 'feat'))
Inputs may be any that keep to these rules, and one draw needn't show every extreme that they name: `expert_ids`: each token names two different experts of 0 to 7. Among the 8 tokens of one device, each expert below 2 is named by at most 4 tokens; in every draw one of these experts, drawn from the seed and the same for all devices, is named by exactly 4 tokens of every device.
All inputs are finite; a program needn't handle non-finite values.
Results may differ from a plain program's by a relative error of at most 0.0021.
Values may be sent and summed in bfloat16 or wider, within the bound.
A program may use at most 128 MiB of HBM per device.

v0:
```python
import jax
import jax.numpy as jnp
from jax import lax
from jax.sharding import PartitionSpec as P

sharpness = 0.1
kernel_width = 0.5
density_weight = 0.01
highest = lax.Precision.HIGHEST


def partner(block, axis, stride):
    count = lax.axis_size(axis)
    route = []
    for low in range(count):
        high = low | 1 << stride
        if high != low and high < count:
            route += [(low, high), (high, low)]
    return lax.ppermute(block, axis, route)


def pack_slots(tokens, expert_ids, route_weights, experts):
    capacity = tokens.shape[0] // 2
    window = jnp.arange(experts, dtype=jnp.int32)
    matches = expert_ids[:, :, None] == window[None, None, :]
    named = jnp.sum(matches.astype(jnp.int32), axis=1)
    weighted = jnp.sum(
        jnp.where(matches, route_weights[:, :, None], jnp.zeros((), jnp.bfloat16)), axis=1
    )
    slot_index = jnp.cumsum(named, axis=0) - named
    places = jnp.arange(capacity, dtype=jnp.int32)
    chosen = (named.T[:, None, :] == 1) & (slot_index.T[:, None, :] == places[None, :, None])
    slot_rows = jnp.einsum(
        "ect,td->ecd", chosen.astype(jnp.bfloat16), tokens, preferred_element_type=jnp.float32
    ).astype(jnp.bfloat16)
    slot_weights = jnp.sum(
        jnp.where(chosen, weighted.T[:, None, :], jnp.zeros((), jnp.bfloat16)), axis=2
    )
    return (slot_rows, slot_weights)


def contract_rows(left, right):
    return lax.dot_general(left, right, (((0,), (0,)), ((), ())), precision=highest)


def body(
    tokens,
    expert_ids,
    route_weights,
    gate_proj,
    up_proj,
    down_proj,
    enc_weight,
    enc_bias,
    log_threshold,
    dec_weight,
):
    copies = 2
    experts = lax.axis_size("expert") // copies
    slot_rows, slot_weights = pack_slots(tokens, expert_ids, route_weights, experts)
    send_rows = jnp.repeat(slot_rows, copies, axis=0)
    send_weights = jnp.repeat(slot_weights, copies, axis=0)
    came_rows, came_weights = (
        lax.all_to_all(send_rows, "expert", split_axis=0, concat_axis=0, tiled=True),
        lax.all_to_all(send_weights, "expert", split_axis=0, concat_axis=0, tiled=True),
    )
    all_rows, all_weights = (
        lax.all_gather(came_rows, "feat", axis=0, tiled=True),
        lax.all_gather(came_weights, "feat", axis=0, tiled=True),
    )
    width = tokens.shape[1]
    token_rows = all_rows.reshape(-1, width)
    row_weights = all_weights.reshape(-1).astype(jnp.float32)
    gate_act = jnp.dot(token_rows, gate_proj, preferred_element_type=jnp.float32)
    up_act = jnp.dot(token_rows, up_proj, preferred_element_type=jnp.float32)
    hidden = (jax.nn.silu(gate_act) * up_act).astype(jnp.bfloat16)
    target_part = jnp.dot(hidden, down_proj, preferred_element_type=jnp.float32)
    inputs = token_rows.astype(jnp.float32)
    preact = jnp.dot(inputs, enc_weight, precision=highest) + enc_bias
    threshold = jnp.exp(log_threshold)
    shifted = preact - threshold
    soft_gate = jax.nn.sigmoid(shifted / sharpness)
    active = preact * soft_gate
    partial_error = jnp.dot(active, dec_weight, precision=highest) - target_part
    feat_total = lax.psum(partial_error, "feat")
    recon_error = feat_total + partner(feat_total, "expert", 0)
    residual_grad = 2.0 * row_weights[:, None] * recon_error
    grad_decoder = contract_rows(active, residual_grad)
    grad_active = lax.dot_general(
        residual_grad, dec_weight, (((1,), (1,)), ((), ())), precision=highest
    )
    grad_pre = grad_active * soft_gate
    grad_encoder = contract_rows(inputs, grad_pre)
    grad_bias = jnp.sum(grad_pre, axis=0)
    kernel = jnp.maximum(0.0, 1.0 - jnp.abs(shifted) / kernel_width) / kernel_width
    slope_sum = jnp.sum(
        (grad_active * threshold + density_weight * row_weights[:, None]) * kernel, axis=0
    )
    grad_threshold = -threshold * slope_sum
    return (grad_encoder, grad_decoder, grad_bias, grad_threshold)


def solution(mesh):
    in_specs = (
        P(("expert", "feat"), None),
        P(("expert", "feat"), None),
        P(("expert", "feat"), None),
        P(None, ("expert", "feat")),
        P(None, ("expert", "feat")),
        P(("expert", "feat"), None),
        P(None, ("expert", "feat")),
        P(("expert", "feat")),
        P(("expert", "feat")),
        P(("expert", "feat"), None),
    )
    out_specs = (
        P(None, ("expert", "feat")),
        P(("expert", "feat"), None),
        P(("expert", "feat")),
        P(("expert", "feat")),
    )
    return jax.shard_map(body, mesh=mesh, in_specs=in_specs, out_specs=out_specs, check_vma=False)
```

profile of v0, /device:TPU:1, one launch (start us, length us, event | category | flops | bytes accessed | tf_op | source)
XLA Modules:
  0.0 474.6 jit_solution(3377354966974964132)
XLA Ops:
  7.2 0.8 convert_reduce_fusion
  8.1 0.2 reduce_window_sum.11
  8.2 1.0 convolution_convert_fusion
  9.3 9.7 %all_to_all.17 = bf16[4,4,4096]{2,1,0:T(4,128)(2,1)} all-to-all(bf16[4,4,4096]{2,1,0:T(4,128)(2,1)S(1)} %bitcast.20), channel_id=1, replica_groups=mesh['expert'=4,'feat'=32] {'expert'}, dimensions={0} | all-to-all | bytes 262144 | tf_op jit(solution)/shard_map/all_to_all | solution.py:64
  19.0 0.0 all-reduce.2.cloned.1.call-start
  19.1 0.7 exp.10
  19.8 48.0 %all-gather.3.cloned.1.call-done = bf16[128,4,4096]{2,1,0:T(4,128)(2,1)} async-done(((bf16[4,4,4096]{2,1,0:T(4,128)(2,1)}), bf16[128,4,4096]{2,1,0:T(4,128)(2,1)}) %all-gather.3.cloned.1.call-update) | async-done | bytes 4194320 | tf_op jit(solution)/shard_map/all_gather | solution.py:68
  67.8 6.9 %reshape.45 = bf16[512,4096]{1,0:T(8,128)(2,1)} reshape(bf16[128,4,4096]{2,1,0:T(4,128)(2,1)} %all-gather.3.cloned.1.call-done) | data formatting | bytes 8388608 | tf_op jit(solution)/shard_map/reshape | solution.py:72
  74.7 4.3 fusion.31
  79.0 5.8 %convolution_add_fusion = f32[512,256]{1,0:T(8,128)S(1)} fusion(bf16[512,4096]{1,0:T(8,128)(2,1)S(1)} %copy-done.1, f32[4096,256]{1,0:T(8,128)} %param.16, f32[256]{0:T(256)S(1)} %copy-done.7), kind=kOutput, calls=%fused_computation.6 | convolution fusion | flops 6442582016 | bytes 8913920 | tf_op jit(solution)/shard_map/dot_general | solution.py:79
  84.9 8.7 %fusion.3 = f32[512,4096]{1,0:T(8,128)} fusion(bf16[224,4096]{1,0:T(8,128)(2,1)S(1)} %copy-done, bf16[512,4096]{1,0:T(8,128)(2,1)} %reshape.45, bf16[4096,224]{0,1:T(8,128)(2,1)} %param.14, f32[512,224]{0,1:T(8,128)S(1)} %fusion.31), kind=kOutput, calls=%fused_computation.8 | convolution fusion | flops 1879736320 | bytes 16711680 | tf_op jit(solution)/shard_map/dot_general | solution.py:77
  93.6 13.0 %convolution_subtract_fusion = f32[512,4096]{1,0:T(8,128)} fusion(f32[512,4096]{1,0:T(8,128)} %fusion.3, f32[256,4096]{1,0:T(8,128)} %param.19, f32[512,256]{1,0:T(8,128)S(1)} %convolution_add_fusion, f32[256]{0:T(256)S(1)} %exp.10), kind=kOutput, calls=%fused_computation.1 | convolution fusion | flops 6445334528 | bytes 21496832 | tf_op jit(solution)/shard_map/dot_general | solution.py:84
  106.6 119.7 %all-reduce.2.cloned.1.call-done = f32[512,4096]{1,0:T(8,128)} async-done(((f32[512,4096]{1,0:T(8,128)}), f32[512,4096]{1,0:T(8,128)}) %all-reduce.2.cloned.1.call-update) | async-done | bytes 8388624 | tf_op jit(solution)/shard_map/psum | solution.py:85
  226.4 1.2 collective-permute-start
  227.6 0.1 fusion.18
  227.7 181.8 %all_to_all.18 = bf16[4,1,4]{2,1,0:T(2,128)(2,1)S(1)} all-to-all(bf16[4,1,4]{2,1,0:T(2,128)(2,1)S(1)} %copy.21), channel_id=1, replica_groups=mesh['expert'=4,'feat'=32] {'expert'}, dimensions={0} | all-to-all | bytes 64 | tf_op jit(solution)/shard_map/all_to_all | solution.py:65
  409.5 26.1 %all-gather = bf16[128,1,4]{2,1,0:T(2,128)(2,1)S(1)} all-gather(bf16[4,1,4]{2,1,0:T(2,128)(2,1)S(1)} %all_to_all.18), channel_id=2, replica_groups=mesh['expert'=4,'feat'=32] {'feat'}, dimensions={0}, use_global_device_ids=true | all-gather | bytes 1056 | tf_op jit(solution)/shard_map/all_gather | solution.py:69
  435.6 0.4 multiply_reduce_fusion.1
  436.0 0.1 mul.73
  436.1 0.1 mul.63
  436.2 13.2 %multiply_reduce_fusion = (f32[256]{0:T(256)S(1)}, f32[256]{0:T(256)}, f32[512,256]{1,0:T(8,128)S(1)}) fusion(f32[512,256]{1,0:T(8,128)S(1)} %convolution_add_fusion, f32[512]{0:T(512)S(1)} %mul.73, f32[256]{0:T(256)S(1)} %exp.10, f32[256,4096]{1,0:T(8,128)} %param.19, f32[512,4096]{1,0:T(8,128)} %all-reduce.2.cloned.1.call-done, ...), kind=kOutput, calls=%fused_computation.9 | convolution fusion | flops 6448741888 | bytes 22027264 | tf_op jit(solution)/shard_map/dot_general | solution.py:89
  449.4 6.3 %fusion.29 = f32[4096,256]{1,0:T(8,128)} fusion(bf16[512,4096]{1,0:T(8,128)(2,1)S(1)} %copy-done.2, f32[512,256]{1,0:T(8,128)S(1)} %get-tuple-element.8, f32[512,256]{1,0:T(8,128)S(1)} %convolution_add_fusion, f32[256]{0:T(256)S(1)} %exp.10), kind=kOutput, calls=%fused_computation.41 | convolution fusion | flops 6443237376 | bytes 9438208 | tf_op jit(solution)/shard_map/dot_general | solution.py:43
  455.7 0.6 negate_multiply_fusion
  456.3 11.5 %fusion = f32[256,4096]{1,0:T(8,128)} fusion(f32[512,4096]{1,0:T(8,128)S(1)} %copy-done.3, f32[512,4096]{1,0:T(8,128)} %collective-permute-done, f32[512]{0:T(512)S(1)} %mul.63, f32[512,256]{1,0:T(8,128)S(1)} %convolution_add_fusion, f32[256]{0:T(256)S(1)} %exp.10), kind=kOutput, calls=%fused_computation.4 | convolution fusion | flops 6447431680 | bytes 21498880 | tf_op jit(solution)/shard_map/dot_general | solution.py:43
  (26 shorter events, 0.2 us)
Async XLA Ops:
  7.2 77.7 %copy-start = (bf16[224,4096]{1,0:T(8,128)(2,1)S(1)}, bf16[224,4096]{1,0:T(8,128)(2,1)}, u32[]{:S(2)}) copy-start(bf16[224,4096]{1,0:T(8,128)(2,1)} %param.15) | copy-start | bytes 5505028
  7.2 60.6 %all-gather.3.cloned.1.call-start = ((), (), s32[]{:S(2)}) async-start(), calls=%async_computation.2 | async-start | bytes 4325376 | tf_op jit(solution)/shard_map/all_gather | solution.py:68
  19.0 207.3 %all-reduce.2.cloned.1.call-start = ((), (), s32[]{:S(2)}) async-start(), calls=%async_computation.3 | async-start | bytes 16777216 | tf_op jit(solution)/shard_map/psum | solution.py:85
  74.7 4.4 copy-start.1
  74.7 4.4 copy-start.7
  106.6 121.0 %copy-start.5 = (s32[8,2]{0,1:T(2,128)S(1)}, s32[8,2]{0,1:T(2,128)}, u32[]{:S(2)}) copy-start(s32[8,2]{0,1:T(2,128)} %param.11) | copy-start | bytes 196
  106.6 121.0 %copy-start.6 = (bf16[8,2]{0,1:T(2,128)(2,1)S(1)}, bf16[8,2]{0,1:T(2,128)(2,1)}, u32[]{:S(2)}) copy-start(bf16[8,2]{0,1:T(2,128)(2,1)} %param.12) | copy-start | bytes 100
  226.4 209.8 %collective-permute-start = (f32[512,4096]{1,0:T(8,128)}, f32[512,4096]{1,0:T(8,128)}, u32[]{:S(2)}, u32[]{:S(2)}) collective-permute-start(f32[512,4096]{1,0:T(8,128)} %all-reduce.2.cloned.1.call-done), channel_id=1, source_target_pairs={{0,32},{32,0},{64,96},{96,64},{1,33},{33,1},{65,97},{97,65},{2,34}... | collective-permute-start | bytes 25165832 | tf_op jit(solution)/shard_map/ppermute | solution.py:19
  436.2 13.2 %copy-start.2 = (bf16[512,4096]{1,0:T(8,128)(2,1)S(1)}, bf16[512,4096]{1,0:T(8,128)(2,1)}, u32[]{:S(2)}) copy-start(bf16[512,4096]{1,0:T(8,128)(2,1)} %reshape.45) | copy-start | bytes 12582916
  449.4 6.3 %copy-start.4 = (f32[256]{0:T(256)S(1)}, f32[256]{0:T(256)}, u32[]{:S(2)}) copy-start(f32[256]{0:T(256)} %param.18) | copy-start | bytes 3076
  449.4 6.9 %copy-start.3 = (f32[512,4096]{1,0:T(8,128)S(1)}, f32[512,4096]{1,0:T(8,128)}, u32[]{:S(2)}) copy-start(f32[512,4096]{1,0:T(8,128)} %all-reduce.2.cloned.1.call-done) | copy-start | bytes 25165828
Sparse Core Ops, SparseCore 0:
  19.2 48.5 all-gather.2
  106.8 119.5 all-reduce.1
where the time goes:
time: 475 us
  blocking collectives  218 us (46%)
  waiting for transfers between devices  168 us (35%)
  matrix products  63.9 us (13%)
  between operations  14.1 us (3%)
  local copies, waits for them, and re-layouts  7.86 us (2%)
    all_to_all x1, blocking collectives, body(): lax.all_to_all(send_weights, 'expert', split_axis=0, concat_axis=0, tiled...  182 us
    psum x1, waiting for transfers between devices, body(): feat_total = lax.psum(partial_error, 'feat')  120 us
    all_gather x1, waiting for transfers between devices, body(): lax.all_gather(came_rows, 'feat', axis=0, tiled=True)  48 us
    all_gather x1, blocking collectives, body(): lax.all_gather(came_weights, 'feat', axis=0, tiled=True)  26.1 us
    dot_general x2, matrix products, contract_rows(): lax.dot_general(left, right, (((0,), (0,)), ((), ())), precision=highest)  17.8 us
    dot_general x1, matrix products, body(): lax.dot_general(residual_grad, dec_weight, (((1,), (1,)), ((), ())), prec...  13.2 us
    dot_general x1, matrix products, body(): partial_error = jnp.dot(active, dec_weight, precision=highest) - target_part  13 us
    all_to_all x1, blocking collectives, body(): lax.all_to_all(send_rows, 'expert', split_axis=0, concat_axis=0, tiled=True)  9.75 us
  transfers between devices with their start and end apart: 3, of which 2 were waited for; matrix products, arithmetic and copies ran while one was open for 0% of the time, Pallas kernels for 0%

commit v1 on v0

--- a/solution.py
+++ b/solution.py
@@ -82,7 +82,11 @@
     soft_gate = jax.nn.sigmoid(shifted / sharpness)
     active = preact * soft_gate
     partial_error = jnp.dot(active, dec_weight, precision=highest) - target_part
-    feat_total = lax.psum(partial_error, "feat")
+    feat_total = partial_error
+    for hop in (1, 2, 4, 8, 16):
+        feat_total = feat_total + lax.ppermute(
+            feat_total, "feat", [(dev, dev ^ hop) for dev in range(32)]
+        )
     recon_error = feat_total + partner(feat_total, "expert", 0)
     residual_grad = 2.0 * row_weights[:, None] * recon_error
     grad_decoder = contract_rows(active, residual_grad)

time: 475 us -> 1150 us (2.42)
  waiting for transfers between devices: 168 us -> 782 us
  other arithmetic: 2.08 us -> 57.7 us
    ppermute x0 -> x5, waiting for transfers between devices: none -> 733 us  [body(): lax.ppermute(feat_total, 'feat', [(dev, dev ^ hop) for dev in range(32)])]
    psum x1 -> x0, waiting for transfers between devices: 120 us -> none  [body(): feat_total = lax.psum(partial_error, 'feat')]
    add x0 -> x5, other arithmetic: none -> 55.7 us  [body(): feat_total + lax.ppermute(feat_total, 'feat', [(dev, dev ^ hop) for dev i...]
  transfers between devices with their start and end apart: 3 -> 7, of which waited for: 2 -> 6; matrix products, arithmetic and copies ran while one was open for 0% -> 0% of each run, Pallas kernels for 0% -> 0%
where the time goes in v1:
time: 1150 us
  waiting for transfers between devices  782 us (68%)
  blocking collectives  217 us (19%)
  matrix products  61.6 us (5%)
  other arithmetic  57.7 us (5%)
  between operations  14.1 us (1%)
    ppermute x5, waiting for transfers between devices, body(): lax.ppermute(feat_total, 'feat', [(dev, dev ^ hop) for dev in range(32)])  733 us
    all_to_all x1, blocking collectives, body(): lax.all_to_all(send_weights, 'expert', split_axis=0, concat_axis=0, tiled...  179 us
    add x5, other arithmetic, body(): feat_total + lax.ppermute(feat_total, 'feat', [(dev, dev ^ hop) for dev i...  55.7 us
    all_gather x1, waiting for transfers between devices, body(): lax.all_gather(came_rows, 'feat', axis=0, tiled=True)  48.1 us
    all_gather x1, blocking collectives, body(): lax.all_gather(came_weights, 'feat', axis=0, tiled=True)  28.6 us
  transfers between devices with their start and end apart: 7, of which 6 were waited for; matrix products, arithmetic and copies ran while one was open for 0% of the time, Pallas kernels for 0%

profile of v1, /device:TPU:1, one launch (start us, length us, event | category | flops | bytes accessed | tf_op | source)
XLA Modules:
  0.0 1150.2 jit_solution(7684335809899829852)
XLA Ops:
  9.3 9.7 all_to_all.17
  19.7 48.1 %all-gather.3.cloned.1.call-done = bf16[128,4,4096]{2,1,0:T(4,128)(2,1)} async-done(((bf16[4,4,4096]{2,1,0:T(4,128)(2,1)}), bf16[128,4,4096]{2,1,0:T(4,128)(2,1)}) %all-gather.3.cloned.1.call-update) | async-done | bytes 4194320 | tf_op jit(solution)/shard_map/all_gather | solution.py:68
  67.8 6.9 reshape.45
  74.7 4.3 fusion.31
  79.0 5.8 convolution_add_fusion
  84.9 8.7 fusion.3
  93.6 10.6 convolution_subtract_fusion
  104.2 3.2 copy-done.5
  107.7 13.0 %collective-permute-done = f32[512,4096]{1,0:T(8,128)} collective-permute-done((f32[512,4096]{1,0:T(8,128)S(1)}, f32[512,4096]{1,0:T(8,128)}, u32[]{:S(2)}, u32[]{:S(2)}) %collective-permute-start) | collective-permute-done | bytes 8388640 | tf_op jit(solution)/shard_map/ppermute | solution.py:87
  120.7 11.1 add.45
  132.7 181.2 %collective-permute-done.1 = f32[512,4096]{1,0:T(8,128)} collective-permute-done((f32[512,4096]{1,0:T(8,128)}, f32[512,4096]{1,0:T(8,128)}, u32[]{:S(2)}, u32[]{:S(2)}) %collective-permute-start.1) | collective-permute-done | bytes 8388640 | tf_op jit(solution)/shard_map/ppermute | solution.py:87
  314.0 11.1 add.46
  325.1 2.1 collective-permute-start.2
  327.2 180.6 %collective-permute-done.2 = f32[512,4096]{1,0:T(8,128)} collective-permute-done((f32[512,4096]{1,0:T(8,128)}, f32[512,4096]{1,0:T(8,128)}, u32[]{:S(2)}, u32[]{:S(2)}) %collective-permute-start.2) | collective-permute-done | bytes 8388640 | tf_op jit(solution)/shard_map/ppermute | solution.py:87
  507.8 11.1 add.47
  519.6 179.6 %collective-permute-done.3 = f32[512,4096]{1,0:T(8,128)} collective-permute-done((f32[512,4096]{1,0:T(8,128)}, f32[512,4096]{1,0:T(8,128)}, u32[]{:S(2)}, u32[]{:S(2)}) %collective-permute-start.3) | collective-permute-done | bytes 8388640 | tf_op jit(solution)/shard_map/ppermute | solution.py:87
  699.2 11.1 add.48
  712.1 179.1 %collective-permute-done.4 = f32[512,4096]{1,0:T(8,128)} collective-permute-done((f32[512,4096]{1,0:T(8,128)}, f32[512,4096]{1,0:T(8,128)}, u32[]{:S(2)}, u32[]{:S(2)}) %collective-permute-start.4) | collective-permute-done | bytes 8388640 | tf_op jit(solution)/shard_map/ppermute | solution.py:87
  891.2 11.1 add.49
  903.7 178.7 %all_to_all.18 = bf16[4,1,4]{2,1,0:T(2,128)(2,1)S(1)} all-to-all(bf16[4,1,4]{2,1,0:T(2,128)(2,1)S(1)} %copy.21), channel_id=1, replica_groups=mesh['expert'=4,'feat'=32] {'expert'}, dimensions={0} | all-to-all | bytes 64 | tf_op jit(solution)/shard_map/all_to_all | solution.py:65
  1082.4 28.6 %all-gather = bf16[128,1,4]{2,1,0:T(2,128)(2,1)S(1)} all-gather(bf16[4,1,4]{2,1,0:T(2,128)(2,1)S(1)} %all_to_all.18), channel_id=2, replica_groups=mesh['expert'=4,'feat'=32] {'feat'}, dimensions={0}, use_global_device_ids=true | all-gather | bytes 1056 | tf_op jit(solution)/shard_map/all_gather | solution.py:69
  1111.6 13.2 %multiply_reduce_fusion = (f32[256]{0:T(256)S(1)}, f32[256]{0:T(256)}, f32[512,256]{1,0:T(8,128)S(1)}) fusion(f32[512,256]{1,0:T(8,128)S(1)} %convolution_add_fusion, f32[512]{0:T(512)S(1)} %mul.73, f32[256]{0:T(256)S(1)} %exp.10, f32[256,4096]{1,0:T(8,128)} %param.19, f32[512,4096]{1,0:T(8,128)} %add.49, f32[512,4096]{1,0:T(8,128)} %collective-permute-done.5, ...), kind=kOutput, calls=%fused_computation.9 | convolution fusion | flops 6448741888 | bytes 22027264 | tf_op jit(solution)/shard_map/dot_general | solution.py:93
  1124.8 6.3 fusion.29
  1131.7 11.6 %fusion = f32[256,4096]{1,0:T(8,128)} fusion(f32[512,4096]{1,0:T(8,128)S(1)} %copy-done.2, f32[512,4096]{1,0:T(8,128)} %collective-permute-done.5, f32[512]{0:T(512)S(1)} %mul.63, f32[512,256]{1,0:T(8,128)S(1)} %convolution_add_fusion, f32[256]{0:T(256)S(1)} %exp.10), kind=kOutput, calls=%fused_computation.4 | convolution fusion | flops 6447431680 | bytes 21498880 | tf_op jit(solution)/shard_map/dot_general | solution.py:43
  (42 shorter events, 9.0 us)
Async XLA Ops:
  7.2 77.7 %copy-start = (bf16[224,4096]{1,0:T(8,128)(2,1)S(1)}, bf16[224,4096]{1,0:T(8,128)(2,1)}, u32[]{:S(2)}) copy-start(bf16[224,4096]{1,0:T(8,128)(2,1)} %param.15) | copy-start | bytes 5505028
  7.2 60.6 %all-gather.3.cloned.1.call-start = ((), (), s32[]{:S(2)}) async-start(), calls=%async_computation.2 | async-start | bytes 4325376 | tf_op jit(solution)/shard_map/all_gather | solution.py:68
  74.7 4.3 copy-start.3
  74.7 4.4 copy-start.9
  104.2 3.2 copy-start.5
  107.4 13.3 %collective-permute-start = (f32[512,4096]{1,0:T(8,128)S(1)}, f32[512,4096]{1,0:T(8,128)}, u32[]{:S(2)}, u32[]{:S(2)}) collective-permute-start(f32[512,4096]{1,0:T(8,128)S(1)} %convolution_subtract_fusion), channel_id=1, source_target_pairs={{0,1},{1,0},{2,3},{3,2},{4,5},{5,4},{6,7},{7,6},{8,9},{9,8},{10,11... | collective-permute-start | bytes 25165832 | tf_op jit(solution)/shard_map/ppermute | solution.py:87
  131.8 182.1 %collective-permute-start.1 = (f32[512,4096]{1,0:T(8,128)}, f32[512,4096]{1,0:T(8,128)}, u32[]{:S(2)}, u32[]{:S(2)}) collective-permute-start(f32[512,4096]{1,0:T(8,128)} %add.45), channel_id=1, source_target_pairs={{0,2},{1,3},{2,0},{3,1},{4,6},{5,7},{6,4},{7,5},{8,10},{9,11},{10,... | collective-permute-start | bytes 25165832 | tf_op jit(solution)/shard_map/ppermute | solution.py:87
  325.1 182.7 %collective-permute-start.2 = (f32[512,4096]{1,0:T(8,128)}, f32[512,4096]{1,0:T(8,128)}, u32[]{:S(2)}, u32[]{:S(2)}) collective-permute-start(f32[512,4096]{1,0:T(8,128)} %add.46), channel_id=1, source_target_pairs={{0,4},{1,5},{2,6},{3,7},{4,0},{5,1},{6,2},{7,3},{8,12},{9,13},{10,... | collective-permute-start | bytes 25165832 | tf_op jit(solution)/shard_map/ppermute | solution.py:87
  518.9 180.3 %collective-permute-start.3 = (f32[512,4096]{1,0:T(8,128)}, f32[512,4096]{1,0:T(8,128)}, u32[]{:S(2)}, u32[]{:S(2)}) collective-permute-start(f32[512,4096]{1,0:T(8,128)} %add.47), channel_id=1, source_target_pairs={{0,8},{1,9},{2,10},{3,11},{4,12},{5,13},{6,14},{7,15},{8,0},{9,1},... | collective-permute-start | bytes 25165832 | tf_op jit(solution)/shard_map/ppermute | solution.py:87
  710.3 193.2 %copy-start.7 = (s32[8,2]{0,1:T(2,128)S(1)}, s32[8,2]{0,1:T(2,128)}, u32[]{:S(2)}) copy-start(s32[8,2]{0,1:T(2,128)} %param.11) | copy-start | bytes 196
  710.3 193.2 %copy-start.8 = (bf16[8,2]{0,1:T(2,128)(2,1)S(1)}, bf16[8,2]{0,1:T(2,128)(2,1)}, u32[]{:S(2)}) copy-start(bf16[8,2]{0,1:T(2,128)(2,1)} %param.12) | copy-start | bytes 100
  710.3 180.9 %collective-permute-start.4 = (f32[512,4096]{1,0:T(8,128)}, f32[512,4096]{1,0:T(8,128)}, u32[]{:S(2)}, u32[]{:S(2)}) collective-permute-start(f32[512,4096]{1,0:T(8,128)} %add.48), channel_id=1, source_target_pairs={{0,16},{1,17},{2,18},{3,19},{4,20},{5,21},{6,22},{7,23},{8,24},{9,... | collective-permute-start | bytes 25165832 | tf_op jit(solution)/shard_map/ppermute | solution.py:87
  902.3 209.3 %collective-permute-start.5 = (f32[512,4096]{1,0:T(8,128)}, f32[512,4096]{1,0:T(8,128)}, u32[]{:S(2)}, u32[]{:S(2)}) collective-permute-start(f32[512,4096]{1,0:T(8,128)} %add.49), channel_id=1, source_target_pairs={{0,32},{32,0},{64,96},{96,64},{1,33},{33,1},{65,97},{97,65},{2,34}... | collective-permute-start | bytes 25165832 | tf_op jit(solution)/shard_map/ppermute | solution.py:19
  1111.6 13.2 %copy-start.4 = (bf16[512,4096]{1,0:T(8,128)(2,1)S(1)}, bf16[512,4096]{1,0:T(8,128)(2,1)}, u32[]{:S(2)}) copy-start(bf16[512,4096]{1,0:T(8,128)(2,1)} %reshape.45) | copy-start | bytes 12582916
  1124.8 6.3 copy-start.6
  1124.8 6.9 copy-start.2
  1131.7 11.7 %copy-start.1 = (bf16[224,4096]{1,0:T(8,128)(2,1)S(1)}, bf16[224,4096]{1,0:T(8,128)(2,1)}, u32[]{:S(2)}) copy-start(bf16[224,4096]{1,0:T(8,128)(2,1)} %param.15) | copy-start | bytes 5505028
Sparse Core Ops, SparseCore 0:
  19.2 48.5 all-gather.2
